TPU v7x, 32 devices: a whole 2x2x4 slice. The times are simulated.
32 devices in a mesh: groups: 2 (over x), seq: 16 (over z, y, core).
Axes of the slice: x: 2, y: 2, z: 4, core: 2. Of those that a mesh axis runs over, the one named last changes fastest.
Arguments:
- cache_keys: bfloat16 [131072, 1024], P(('groups', 'seq')), parts along dimension 0, may hold values from -48 to 48
- cache_values: bfloat16 [131072, 1024], P(('groups', 'seq')), parts along dimension 0, may hold values from -6 to 6
- sketch_matrix: float32 [1024, 160], replicated, may hold values from -6 to 6
- queries: bfloat16 [6, 8192], P('groups'), parts along dimension 0, may hold values from -2000 to 2000
- fresh_keys: bfloat16 [6, 1024], P('groups'), parts along dimension 0, may hold values from -20 to 20
- fresh_values: bfloat16 [6, 1024], P('groups'), parts along dimension 0, may hold values from -6 to 6
- chosen: int32 [6, 8, 256], P('groups'), parts along dimension 0, may hold values from 0 to 8191, as said below
- shard_counts: int32 [6, 8, 16], P('groups'), parts along dimension 0, may hold values from 0 to 48, as said below
- outliers: int32 [64], P('groups'), parts along dimension 0, may hold values from 0 to 8191, as said below
Outputs:
- attended: bfloat16 [6, 8192], P('groups', 'seq'), parts along dimension 0
- key_factor: float32 [131072, 160], P(('groups', 'seq')), parts along dimension 0
There are 2 independent parts, one for each index of `groups`. A program takes and returns all parts, laid end to end along the dimension named above; an argument that names none is the same for every part. Nothing has to cross between parts.
Inputs may be any that keep to these rules, and one draw needn't show every extreme that they name: Each list chosen[t, g] holds distinct span numbers in ascending order, none of them an outlier span; shard s holds spans s * 512 to (s+1) * 512 - 1. shard_counts[t, g, s] is the number of entries of chosen[t, g] on shard s; they sum to 256; the most is 48, reached in every list. `outliers`: distinct span numbers in ascending order; at most 4 on one shard, reached on some shard.
All inputs are finite; a program needn't handle non-finite values.
Results may differ from a plain program's by a relative error of at most 0.0228.
Values may be sent and summed in bfloat16 or wider, within the bound.
No kernel may reach another device: no remote copies, remote signals or barrier semaphores. Data moves between devices by JAX's collectives and lax.ppermute only.
A program may use at most 128 MiB of HBM per device.

v0:
```python
import jax
import jax.numpy as jnp
from jax import lax
from jax.sharding import PartitionSpec as P

KVH = 8
HD = 128
QH = 64
SPAN = 8
OMOST = 4


def merged_2(x, axis, combine):
    everything = jax.tree.map(lambda part: lax.all_gather(part, axis), x)
    leading = jax.tree.map(lambda part: part[0], everything)

    def step(k, so_far):
        return combine(so_far, jax.tree.map(lambda part: part[k], everything))

    return lax.fori_loop(1, lax.axis_size(axis), step, leading)


def rotate(vectors, positions):
    half_width = vectors.shape[-1] // 2
    exponents = jnp.arange(half_width, dtype=jnp.float32) * (2.0 / vectors.shape[-1])
    inverse_freq = jnp.exp(-jnp.log(jnp.float32(500000.0)) * exponents)
    angles = positions.astype(jnp.float32)[..., None] * inverse_freq
    cosine = jnp.cos(angles)
    sine = jnp.sin(angles)
    first_half = vectors[..., :half_width]
    second_half = vectors[..., half_width:]
    return jnp.concatenate(
        [first_half * cosine - second_half * sine, second_half * cosine + first_half * sine],
        axis=-1,
    )


def make_basis(sketch):
    small_gram = jnp.dot(sketch.T, sketch, precision=lax.Precision.HIGHEST)
    lower = jnp.linalg.cholesky(small_gram)
    solved = lax.linalg.triangular_solve(lower, sketch.T, left_side=True, lower=True)
    return solved.T.astype(jnp.bfloat16)


def softmax_part(query_rows, key_rows, value_rows, is_live):
    score_scale = 1.0 / jnp.sqrt(jnp.float32(query_rows.shape[-1]))
    scores = (
        jnp.einsum(
            "...qd,...ld->...ql",
            query_rows,
            key_rows.astype(jnp.float32),
            precision=lax.Precision.HIGHEST,
        )
        * score_scale
    )
    live_mask = is_live[..., None, :]
    scores = jnp.where(live_mask, scores, -1e30)
    run_max = jnp.max(scores, axis=-1)
    weights = jnp.exp(scores - run_max[..., None]) * live_mask
    run_sum = jnp.sum(weights, axis=-1)
    run_out = jnp.einsum(
        "...ql,...ld->...qd",
        weights,
        value_rows.astype(jnp.float32),
        precision=lax.Precision.HIGHEST,
    )
    return (run_max, run_sum, run_out)


def combine(earlier, later):
    joint_max = jnp.maximum(earlier[0], later[0])
    scale_early = jnp.exp(earlier[0] - joint_max)
    scale_late = jnp.exp(later[0] - joint_max)
    return (
        joint_max,
        earlier[1] * scale_early + later[1] * scale_late,
        earlier[2] * scale_early[..., None] + later[2] * scale_late[..., None],
    )


def on_device(
    cache_keys,
    cache_values,
    sketch_matrix,
    queries,
    fresh_keys,
    fresh_values,
    chosen,
    shard_counts,
    outliers,
):
    seq_len, feature_width = cache_keys.shape
    devices = lax.axis_size("seq")
    myself = lax.axis_index("seq")
    length = seq_len * devices
    steps = queries.shape[0]
    group_size = QH // KVH
    per_device = QH // devices
    contract = (((0,), (0,)), ((), ()))
    gram_share = (
        lax.psum_scatter(
            lax.dot_general(cache_keys, cache_keys, contract, preferred_element_type=jnp.float32),
            "seq",
            scatter_dimension=0,
            tiled=True,
        )
        / length
    )
    sketch_share = jnp.dot(gram_share, sketch_matrix, precision=lax.Precision.HIGHEST)
    sketch = lax.all_gather(sketch_share, "seq", axis=0, tiled=True)
    key_basis = make_basis(sketch)
    rank_width = key_basis.shape[1]
    key_factor = jnp.dot(cache_keys, key_basis, preferred_element_type=jnp.float32)
    spans_dev = seq_len // SPAN
    most_slots = 3 * chosen.shape[2] // devices
    preceding = jnp.cumsum(shard_counts, axis=2) - shard_counts
    list_start = lax.dynamic_index_in_dim(preceding, myself, 2, keepdims=False)
    own_count = lax.dynamic_index_in_dim(shard_counts, myself, 2, keepdims=False)
    padded_list = jnp.concatenate([chosen, jnp.zeros((steps, KVH, most_slots), jnp.int32)], axis=2)
    slot_ids = jnp.arange(most_slots, dtype=jnp.int32)
    picked = jnp.take_along_axis(padded_list, list_start[..., None] + slot_ids, axis=2)
    is_live = slot_ids < own_count[..., None]
    shard_base = myself * spans_dev
    local_span = jnp.clip(picked - shard_base, 0, spans_dev - 1)
    factor_spans = key_factor.reshape(spans_dev, SPAN, rank_width)[local_span]
    basis_heads = key_basis.reshape(KVH, HD, rank_width).astype(jnp.float32)
    rebuilt = jnp.einsum(
        "tgmcr,gdr->tgmcd", factor_spans, basis_heads, precision=lax.Precision.HIGHEST
    )
    token_pos = (local_span + shard_base)[..., None] * SPAN + jnp.arange(SPAN, dtype=jnp.int32)
    sel_keys = rotate(rebuilt, token_pos).astype(jnp.bfloat16)
    value_blocks = cache_values.reshape(spans_dev, SPAN, KVH, HD)
    head_ids = jnp.arange(KVH, dtype=jnp.int32)
    sel_values = value_blocks[local_span, :, head_ids[None, :, None], :]
    outlier_here = outliers // spans_dev == myself
    outlier_order = jnp.cumsum(outlier_here.astype(jnp.int32)) - 1
    slot_match = outlier_here[None, :] & (
        outlier_order[None, :] == jnp.arange(OMOST, dtype=jnp.int32)[:, None]
    )
    outlier_local = jnp.sum(jnp.where(slot_match, outliers[None, :] - shard_base, 0), axis=1)
    outlier_live = jnp.any(slot_match, axis=1)
    key_blocks = cache_keys.reshape(spans_dev, SPAN, KVH, HD)
    out_keys = key_blocks[outlier_local[None, :], :, head_ids[:, None], :]
    out_pos = (outlier_local + shard_base)[:, None] * SPAN + jnp.arange(SPAN, dtype=jnp.int32)
    out_keys = rotate(out_keys.astype(jnp.float32), out_pos).astype(jnp.bfloat16)
    out_values = value_blocks[outlier_local[None, :], :, head_ids[:, None], :]
    slot_total = most_slots + OMOST
    slot_keys = jnp.concatenate(
        [sel_keys, jnp.broadcast_to(out_keys[None], (steps, KVH, OMOST, SPAN, HD))], axis=2
    )
    slot_values = jnp.concatenate(
        [sel_values, jnp.broadcast_to(out_values[None], (steps, KVH, OMOST, SPAN, HD))], axis=2
    )
    slot_live = jnp.concatenate(
        [is_live, jnp.broadcast_to(outlier_live[None, None], (steps, KVH, OMOST))], axis=2
    )
    step_pos = length + jnp.arange(steps, dtype=jnp.int32)
    query_rows = rotate(queries.reshape(steps, QH, HD).astype(jnp.float32), step_pos[:, None])
    own_queries = lax.dynamic_slice_in_dim(query_rows, myself * per_device, per_device, 1)
    grouped = query_rows.reshape(steps, KVH, group_size, HD)
    flat_keys = slot_keys.reshape(steps, KVH, slot_total * SPAN, HD)
    flat_values = slot_values.reshape(steps, KVH, slot_total * SPAN, HD)
    token_live = jnp.repeat(slot_live, SPAN, axis=2)
    local_stats = softmax_part(grouped, flat_keys, flat_values, token_live)
    merged = merged_2(local_stats, "seq", combine)
    run_max = lax.dynamic_slice_in_dim(
        merged[0].reshape(steps, QH), myself * per_device, per_device, 1
    )
    run_sum = lax.dynamic_slice_in_dim(
        merged[1].reshape(steps, QH), myself * per_device, per_device, 1
    )
    run_out = lax.dynamic_slice_in_dim(
        merged[2].reshape(steps, QH, HD), myself * per_device, per_device, 1
    )
    own_head = myself * per_device // group_size
    new_keys = lax.dynamic_index_in_dim(
        fresh_keys.reshape(steps, KVH, HD), own_head, 1, keepdims=False
    )
    new_keys = rotate(new_keys.astype(jnp.float32), step_pos).astype(jnp.bfloat16)
    new_values = lax.dynamic_index_in_dim(
        fresh_values.reshape(steps, KVH, HD), own_head, 1, keepdims=False
    )
    score_scale = 1.0 / jnp.sqrt(jnp.float32(HD))
    new_scores = (
        jnp.einsum(
            "thd,sd->ths",
            own_queries,
            new_keys.astype(jnp.float32),
            precision=lax.Precision.HIGHEST,
        )
        * score_scale
    )
    causal = jnp.arange(steps)[None, :] <= jnp.arange(steps)[:, None]
    new_scores = jnp.where(causal[:, None, :], new_scores, -1e30)
    joint_max = jnp.maximum(run_max, jnp.max(new_scores, axis=-1))
    old_scale = jnp.exp(run_max - joint_max)
    new_weights = jnp.exp(new_scores - joint_max[..., None]) * causal[:, None, :]
    summed = run_out * old_scale[..., None] + jnp.einsum(
        "ths,sd->thd", new_weights, new_values.astype(jnp.float32), precision=lax.Precision.HIGHEST
    )
    totals = run_sum * old_scale + jnp.sum(new_weights, axis=-1)
    attended = (summed / totals[..., None]).reshape(steps, per_device * HD).astype(jnp.bfloat16)
    return (attended, key_factor)


def solution(mesh):
    in_specs = (
        P(("groups", "seq"), None),
        P(("groups", "seq"), None),
        P(),
        P("groups", None),
        P("groups", None),
        P("groups", None),
        P("groups", None, None),
        P("groups", None, None),
        P("groups"),
    )
    out_specs = (P("groups", "seq"), P(("groups", "seq"), None))
    return jax.shard_map(
        on_device, mesh=mesh, in_specs=in_specs, out_specs=out_specs, check_vma=False
    )
```

profile of v0, /device:TPU:0, one launch (start us, length us, event | category | flops | bytes accessed | tf_op | source)
XLA Modules:
  0.0 298.9 jit_solution(4955914066819933756)
XLA Ops:
  7.2 15.1 %fusion.89 = f32[1024,1024]{1,0:T(8,128)} fusion(bf16[4096,1024]{1,0:T(8,128)(2,1)} %param.11), kind=kOutput, calls=%fused_computation.175 | convolution fusion | flops 8589934592 | bytes 12582912 | tf_op jit(solution)/shard_map/dot_general | solution.py:102
  23.4 9.1 %gather_fusion.4 = s32[1152]{0:T(1024)S(1)} fusion(s32[3,8,304]{2,1,0:T(8,128)S(1)} %concatenate.47, s32[1152]{0:T(1024)S(1)} %reshape.400), kind=kCustom, calls=%fused_computation.4 | custom fusion | bytes 23040 | tf_op jit(solution)/shard_map/jit(take_along_axis)/gather | solution.py:121
  33.5 4.5 %gather_fusion.1 = bf16[32,8,128]{2,1,0:T(8,128)(2,1)S(1)} fusion(bf16[512,8,8,128]{3,1,2,0:T(8,128)(2,1)} %bitcast.140, s32[32]{0:T(128)S(1)} %reshape.382), kind=kCustom, calls=%fused_computation.1 | custom fusion | bytes 131328 | tf_op jit(solution)/shard_map/gather | solution.py:143
  39.4 5.1 %gather_fusion.3 = bf16[32,8,128]{2,1,0:T(8,128)(2,1)} fusion(bf16[512,8,8,128]{3,1,2,0:T(8,128)(2,1)} %bitcast.145, s32[32]{0:T(128)S(1)} %reshape.382), kind=kCustom, calls=%fused_computation.3 | custom fusion | bytes 131328 | tf_op jit(solution)/shard_map/gather | solution.py:146
  44.5 15.0 %gather_fusion.2 = bf16[1152,8,128]{2,1,0:T(8,128)(2,1)} fusion(bf16[512,8,8,128]{3,1,2,0:T(8,128)(2,1)} %bitcast.146, s32[1152]{0:T(1024)S(1)} %reshape.388), kind=kCustom, calls=%fused_computation.2 | custom fusion | bytes 4727808 | tf_op jit(solution)/shard_map/gather | solution.py:134
  60.1 0.7 fusion.69
  61.4 0.7 subtract_convert_fusion.1
  62.8 35.0 %reduce-scatter.2.cloned.1.call-done = f32[64,1024]{1,0:T(8,128)} async-done(((f32[1024,1024]{1,0:T(8,128)}), f32[64,1024]{1,0:T(8,128)}) %reduce-scatter.2.cloned.1.call-update) | async-done | bytes 262160 | tf_op jit(solution)/shard_map/reduce_scatter | solution.py:101
  97.9 1.7 fusion.36
  99.6 22.6 %all_gather.21 = f32[1024,160]{1,0:T(8,128)S(1)} all-gather(f32[64,160]{1,0:T(8,128)S(1)} %fusion.36), channel_id=1, replica_groups=mesh['groups'=2,'seq'=16] {'seq'}, dimensions={0}, use_global_device_ids=true | all-gather | bytes 696320 | tf_op jit(solution)/shard_map/all_gather | solution.py:110
  122.2 1.9 fusion.90
  124.2 11.7 %cholesky.51 = f32[128,128]{1,0:T(8,128)S(1)} custom-call(f32[128,128]{1,0:T(8,128)S(1)} %cholesky.124), custom_call_target="Cholesky" | custom-call | tf_op jit(solution)/shard_map/jit(cholesky)/cholesky | solution.py:40
  136.0 9.8 %custom-call.14 = f32[1,128,128]{1,2,0:T(8,128)S(1)} custom-call(f32[1,128,128]{2,1,0:T(8,128)S(1)} %get-tuple-element.236), custom_call_target="InvertDiagBlocksLowerTriangular" | custom-call | tf_op jit(solution)/shard_map/jit(cholesky)/cholesky | solution.py:40
  146.1 2.9 cholesky.110
  149.1 0.7 compare_reduce_fusion
  151.8 20.1 %custom-call.15 = f32[2,128,128]{1,2,0:T(8,128)S(1)} custom-call(f32[2,128,128]{2,1,0:T(8,128)S(1)} %pad_maximum_fusion.3), custom_call_target="InvertDiagBlocksLowerTriangular" | custom-call | tf_op jit(solution)/shard_map/triangular_solve | solution.py:41
  172.5 1.0 convolution_subtract_fusion
  173.5 0.6 convolution_convert_fusion
  174.2 6.3 %convolution_bitcast_fusion = f32[4096,160]{0,1:T(8,128)S(1)} fusion(bf16[4096,1024]{1,0:T(8,128)(2,1)} %param.11, bf16[32,1024]{1,0:T(8,128)(2,1)S(1)} %convolution_convert_fusion, bf16[128,1024]{1,0:T(8,128)(2,1)S(1)} %get-tuple-element.249), kind=kOutput, calls=%fused_computation.21 | convolution fusion | flops 1342832640 | bytes 11337728 | tf_op jit(solution)/shard_map/dot_general | solution.py:113
  180.5 0.8 fusion.38
  181.3 3.3 %copy.41 = f32[4096,160]{1,0:T(8,128)} copy(f32[4096,160]{0,1:T(8,128)S(1)} %convolution_bitcast_fusion) | data formatting | bytes 5242880 | tf_op jit(solution)/shard_map/dot_general | solution.py:113
  184.7 1.8 copy.55
  186.4 10.0 %gather_fusion = f32[1152,8,160]{2,1,0:T(8,128)} fusion(f32[512,8,160]{2,1,0:T(8,128)} %bitcast.136, s32[2048]{0:T(1024)} %pad_clamp_fusion), kind=kCustom, calls=%fused_computation | custom fusion | bytes 11801088 | tf_op jit(solution)/shard_map/gather | solution.py:125
  196.4 11.9 %fusion.19 = f32[3,8,48,8,128]{4,2,3,0,1:T(8,128)S(1)} fusion(f32[3,8,48,8,160]{4,3,2,1,0:T(8,128)} %bitcast.137, bf16[8,128,160,1,1]{1,0,2,4,3:T(8,128)(2,1)} %bitcast.143), kind=kOutput, calls=%fused_computation.34 | convolution fusion | flops 2264924160 | bytes 10944512 | tf_op jit(solution)/shard_map/tgmcr,gdr->tgmcd/dot_general | solution.py:127
  208.3 19.4 %fusion.10 = (bf16[3,8,48,8,64]{4,2,3,0,1:T(8,128)(2,1)S(1)}, bf16[3,8,48,8,64]{4,2,3,0,1:T(8,128)(2,1)S(1)}) fusion(f32[3,8,48,8,128]{4,2,3,0,1:T(8,128)S(1)} %fusion.19, f32[64]{0:T(128)S(1)} %multiply_exponential_fusion, f32[3,8,48,8]{2,3,0,1:T(8,128)S(1)} %copy-done.3), kind=kLoop, calls=%fused_computation.23 | loop fusion | flops 5308416 | bytes 7115008 | tf_op jit(solution)/shard_map/convert.11
  227.8 1.4 pad_maximum_fusion
  229.3 3.0 fusion.87
  232.3 2.2 fusion.13
  235.1 18.3 %all-gather.1 = f32[48,8,8]{2,1,0:T(8,128)S(1)} all-gather(f32[3,8,8]{2,1,0:T(8,128)S(1)} %fusion.35), channel_id=3, replica_groups=mesh['groups'=2,'seq'=16] {'seq'}, dimensions={0}, use_global_device_ids=true | all-gather | bytes 13056 | tf_op jit(solution)/shard_map/all_gather | solution.py:14
  253.4 19.3 %all-gather = f32[48,8,8]{2,1,0:T(8,128)S(1)} all-gather(f32[3,8,8]{2,1,0:T(8,128)S(1)} %get-tuple-element.251), channel_id=2, replica_groups=mesh['groups'=2,'seq'=16] {'seq'}, dimensions={0}, use_global_device_ids=true | all-gather | bytes 13056 | tf_op jit(solution)/shard_map/all_gather | solution.py:14
  272.7 0.9 slice.128
  273.6 16.3 %while.21 = (s32[]{:T(128)}, f32[3,8,8]{2,1,0:T(8,128)S(1)}, f32[3,8,8]{2,1,0:T(8,128)S(1)}, f32[3,8,8,128]{3,2,1,0:T(8,128)S(1)}, f32[16,3,8,8]{3,2,1,0:T(8,128...) while((s32[]{:T(128)}, f32[3,8,8]{2,1,0:T(8,128)S(1)}, ...), condition=%wide.region_12.13_spmd, body=%wide.region_11.12_spmd.sunk | while | flops 74885 | bytes 302743 | solution.py:20
  273.6 1.0 fusion.104
  274.7 1.0 fusion.104
  275.8 1.0 fusion.104
  276.9 1.0 fusion.104
  278.0 1.0 fusion.104
  279.1 1.0 fusion.104
  280.2 1.0 fusion.104
  281.3 1.0 fusion.104
  282.4 1.0 fusion.104
  283.4 1.0 fusion.104
  284.5 1.0 fusion.104
  285.6 1.0 fusion.104
  286.7 1.0 fusion.104
  287.8 1.0 fusion.104
  288.9 1.0 fusion.104
  290.3 1.0 fusion.31
  (115 shorter events, 9.2 us)
Async XLA Ops:
  7.2 90.7 %copy-start = (f32[1024,160]{0,1:T(8,128)S(1)}, f32[1024,160]{0,1:T(8,128)}, u32[]{:S(2)}) copy-start(f32[1024,160]{0,1:T(8,128)} %param.13) | copy-start | bytes 1966084
  7.2 15.3 %copy-start.7 = (s32[3,8,16]{2,1,0:T(8,128)S(1)}, s32[3,8,16]{2,1,0:T(8,128)}, u32[]{:S(2)}) copy-start(s32[3,8,16]{2,1,0:T(8,128)} %param.18) | copy-start | bytes 4612
  7.2 16.2 %copy-start.8 = (s32[3,8,256]{2,1,0:T(8,128)S(1)}, s32[3,8,256]{2,1,0:T(8,128)}, u32[]{:S(2)}) copy-start(s32[3,8,256]{2,1,0:T(8,128)} %param.17) | copy-start | bytes 73732
  7.2 90.7 %reduce-scatter.2.cloned.1.call-start = ((), (), s32[]{:S(2)}) async-start(), calls=%async_computation.1 | async-start | bytes 4456448 | tf_op jit(solution)/shard_map/reduce_scatter | solution.py:101
  22.4 250.3 %all-gather.5.cloned.1.call-start = ((), (), s32[]{:S(2)}) async-start(), calls=%async_computation.2 | async-start | bytes 1671168 | tf_op jit(solution)/shard_map/all_gather | solution.py:14
  23.4 9.6 %copy-start.11 = (s32[32]{0:T(128)S(1)}, s32[32]{0:T(128)}, u32[]{:S(2)}) copy-start(s32[32]{0:T(128)} %param.19) | copy-start | bytes 388
  23.4 15.1 %copy-start.6 = (bf16[3,8192]{1,0:T(4,128)(2,1)S(1)}, bf16[3,8192]{1,0:T(4,128)(2,1)}, u32[]{:S(2)}) copy-start(bf16[3,8192]{1,0:T(4,128)(2,1)} %param.14) | copy-start | bytes 147460
  180.5 15.9 %copy-start.1 = (f32[4096,160]{0,1:T(8,128)}, f32[4096,160]{0,1:T(8,128)S(1)}, u32[]{:S(2)}) copy-start(f32[4096,160]{0,1:T(8,128)S(1)} %convolution_bitcast_fusion) | copy-start | bytes 7864324
  196.4 11.9 %copy-start.3 = (f32[3,8,48,8]{2,3,0,1:T(8,128)S(1)}, f32[3,8,48,8]{2,3,0,1:T(8,128)}, u32[]{:S(2)}) copy-start(f32[3,8,48,8]{2,3,0,1:T(8,128)} %add_convert_fusion.1) | copy-start | bytes 110596
  227.8 4.5 %copy-start.4 = (bf16[32,8,128]{2,1,0:T(8,128)(2,1)S(1)}, bf16[32,8,128]{2,1,0:T(8,128)(2,1)}, u32[]{:S(2)}) copy-start(bf16[32,8,128]{2,1,0:T(8,128)(2,1)} %gather_fusion.3) | copy-start | bytes 196612
  227.8 4.5 %copy-start.2 = (bf16[1152,8,128]{2,1,0:T(8,128)(2,1)S(1)}, bf16[1152,8,128]{2,1,0:T(8,128)(2,1)}, u32[]{:S(2)}) copy-start(bf16[1152,8,128]{2,1,0:T(8,128)(2,1)} %gather_fusion.2) | copy-start | bytes 7077892
  227.8 4.5 %copy-start.5 = (f32[3,8,416]{2,1,0:T(8,128)S(1)}, f32[3,8,416]{2,1,0:T(8,128)}, u32[]{:S(2)}) copy-start(f32[3,8,416]{2,1,0:T(8,128)} %convert_element_type.103) | copy-start | bytes 119812
  229.3 5.3 %copy-start.9 = (bf16[3,64]{1,0:T(4,128)(2,1)S(1)}, bf16[3,64]{1,0:T(4,128)(2,1)}, u32[]{:S(2)}) copy-start(bf16[3,64]{1,0:T(4,128)(2,1)} %get-tuple-element.239) | copy-start | bytes 1156
  229.3 5.3 %copy-start.10 = (bf16[3,64]{1,0:T(4,128)(2,1)S(1)}, bf16[3,64]{1,0:T(4,128)(2,1)}, u32[]{:S(2)}) copy-start(bf16[3,64]{1,0:T(4,128)(2,1)} %get-tuple-element.240) | copy-start | bytes 1156
Sparse Core Ops, SparseCore 0:
  22.5 75.3 reduce-scatter.1
  234.7 37.7 all-gather.4
where the time goes:
time: 304 us; the launch traced here: 299 us
  other arithmetic  89.4 us (29%)
  blocking collectives  60.2 us (20%)
  local copies, waits for them, and re-layouts  51.8 us (17%)
  matrix products  45.9 us (15%)
  waiting for transfers between devices  35.1 us (12%)
  between operations  16 us (5%)
    all_gather x2, blocking collectives, merged_2(): everything = jax.tree.map(lambda part: lax.all_gather(part, axis), x)  37.6 us
    reduce_scatter x1, waiting for transfers between devices, on_device(): lax.psum_scatter(lax.dot_general(cache_keys, cache_keys, contract, prefer...  35 us
    another operation x7, other arithmetic, make_basis(): lower = jnp.linalg.cholesky(small_gram)  25.8 us
    all_gather x1, blocking collectives, on_device(): sketch = lax.all_gather(sketch_share, 'seq', axis=0, tiled=True)  22.6 us
    another operation x5, other arithmetic  20.3 us
    another operation x6, other arithmetic, make_basis(): lax.linalg.triangular_solve(lower, sketch.T, left_side=True, lower=True)  20.2 us
    add x15, other arithmetic, combine(): earlier[2] * scale_early[..., None] + later[2] * scale_late[..., None]  15.6 us
    dot_general x1, matrix products, on_device(): lax.dot_general(cache_keys, cache_keys, contract, preferred_element_type=...  15.1 us
  transfers between devices with their start and end apart: 2, of which 1 were waited for; matrix products, arithmetic and copies ran while one was open for 14% of the time, Pallas kernels for 0%

commit v1 on v0

v1 whole, which is shorter than its diff:
```python
import functools

import jax
import jax.numpy as jnp
from jax import lax
from jax.experimental import pallas as pl
from jax.experimental.pallas import tpu as pltpu
from jax.sharding import PartitionSpec as P

KVH = 8
HD = 128
QH = 64
SPAN = 8
OMOST = 4
BF = jnp.bfloat16
F32 = jnp.float32
DEAD = -1e30
LANES = 128
NT = (((1,), (1,)), ((), ()))
TN = (((0,), (0,)), ((), ()))


def vmem():
    return pl.BlockSpec(memory_space=pltpu.VMEM)


def smem():
    return pl.BlockSpec(memory_space=pltpu.SMEM)


def hbm():
    return pl.BlockSpec(memory_space=pl.ANY)


def round_up(x, m):
    return (x + m - 1) // m * m


def split2(x):
    high = x.astype(BF)
    return high, (x - high.astype(F32)).astype(BF)


def split3(x):
    high = x.astype(BF).astype(F32)
    rest = x - high
    middle = rest.astype(BF).astype(F32)
    return high, middle, rest - middle


def sketch_kernel(me_ref, st_ref, keys_hbm, keep_ref, send_ref, keys_ref, acc_ref, sem, *, scale, chunk):
    seq_len = keys_ref.shape[0]
    rank = st_ref.shape[0]
    half = rank // 2
    n = seq_len // chunk
    copies = [
        pltpu.make_async_copy(
            keys_hbm.at[pl.ds(i * chunk, chunk)], keys_ref.at[pl.ds(i * chunk, chunk)], sem.at[i]
        )
        for i in range(n)
    ]
    for c in copies:
        c.start()
    st = st_ref[...].astype(BF)

    def rows(i):
        return keys_ref[i * chunk:(i + 1) * chunk, :]

    def first(i):
        return lax.dot_general(st, rows(i), NT, preferred_element_type=F32).astype(BF)

    def second(i, y):
        return jnp.dot(y, rows(i), preferred_element_type=F32)

    copies[0].wait()
    y = first(0)
    for i in range(1, n):
        copies[i].wait()
        y_next = first(i)
        z = second(i - 1, y)
        if i == 1:
            acc_ref[...] = z
        else:
            acc_ref[...] += z
        y = y_next
    acc_ref[...] = (acc_ref[...] + second(n - 1, y)) * scale
    core = me_ref[0] % 2
    keep_ref[...] = acc_ref[pl.ds(pl.multiple_of(core * half, 8), half), :]
    send_ref[...] = acc_ref[pl.ds(pl.multiple_of((1 - core) * half, 8), half), :]


def sketch_share(me, sketch_t, cache_keys, length):
    seq_len, width = cache_keys.shape
    rank = sketch_t.shape[0]
    chunk = min(512, seq_len)
    half = jax.ShapeDtypeStruct((rank // 2, width), F32)
    return pl.pallas_call(
        functools.partial(sketch_kernel, scale=1.0 / length, chunk=chunk),
        in_specs=[smem(), vmem(), hbm()],
        out_specs=[vmem(), vmem()],
        out_shape=[half, half],
        scratch_shapes=[
            pltpu.VMEM((seq_len, width), BF),
            pltpu.VMEM((rank, width), F32),
            pltpu.SemaphoreType.DMA((seq_len // chunk,)),
        ],
        compiler_params=pltpu.CompilerParams(vmem_limit_bytes=40 << 20),
        name="sketch_share",
    )(me, sketch_t, cache_keys)


def prepare_kernel(
    me_ref, chosen_ref, counts_ref, outl_ref, q_ref, fk_ref, fv_ref, ca_ref, sa_ref, cb_ref, sb_ref, cq_ref, sq_ref,
    keys_hbm, values_hbm,
    slots_ref, live_ref, cc_ref, ss_ref, vg_ref, kx_ref, qs_ref,
    values_ref, okeys_ref, vtmp_ref, xtmp_ref, qtmp_ref, sem, osem, *, most, per_device, tok_sel, tok_main
):
    steps = q_ref.shape[0]
    seq_len = values_ref.shape[0]
    spans = seq_len // SPAN
    me = me_ref[0]
    base = me * spans
    n_chunks = sem.shape[0]
    chunk = seq_len // n_chunks
    copies = [
        pltpu.make_async_copy(
            values_hbm.at[pl.ds(i * chunk, chunk)], values_ref.at[pl.ds(i * chunk, chunk)], sem.at[i]
        )
        for i in range(n_chunks)
    ]
    for c in copies:
        c.start()

    n_out = outl_ref.shape[0]

    def below(i, carry):
        first, here = carry
        s = outl_ref[i]
        return (first + (s < base).astype(jnp.int32), here + ((s >= base) & (s < base + spans)).astype(jnp.int32))

    o_first, o_here = lax.fori_loop(0, n_out, below, (jnp.int32(0), jnp.int32(0)), unroll=8)
    o_span = [
        jnp.clip(outl_ref[jnp.minimum(o_first + j, n_out - 1)] - base, 0, spans - 1) for j in range(OMOST)
    ]
    o_copies = [
        pltpu.make_async_copy(
            keys_hbm.at[pl.ds(pl.multiple_of(o_span[j] // 2 * 16, 16), 16)], okeys_ref.at[j], osem.at[j]
        )
        for j in range(OMOST)
    ]
    for c in o_copies:
        c.start()

    blk = cb_ref.shape[0]
    for a in range(seq_len // blk):
        ca = ca_ref[a:a + 1, :]
        sa = sa_ref[a:a + 1, :]
        cb = cb_ref[...]
        sb = sb_ref[...]
        cc_ref[a * blk:(a + 1) * blk, :] = ca * cb - sa * sb
        ss_ref[a * blk:(a + 1) * blk, :] = sa * cb + ca * sb

    lane = lax.broadcasted_iota(jnp.int32, (8, LANES), 1)
    sign = jnp.where(lane < HD // 2, -1.0, 1.0)

    def turn(x, c, s):
        return x * c + pltpu.roll(x, HD // 2, 1) * (s * sign[:x.shape[0]])

    group = QH // KVH
    n_dest = qs_ref.shape[0]
    rp = qs_ref.shape[1] // 2
    scale = 1.0 / (HD ** 0.5)
    qtmp_ref[...] = jnp.zeros_like(qtmp_ref)
    for t in range(steps):
        c = cq_ref[t:t + 1, :]
        s = sq_ref[t:t + 1, :]
        for h in range(QH):
            x = q_ref[t:t + 1, h * HD:(h + 1) * HD].astype(F32)
            d, i = h // per_device, h % per_device
            r = t * per_device + i
            qtmp_ref[d, r:r + 1, :] = x
        for d in range(n_dest):
            r = t * per_device
            x = qtmp_ref[d, r:r + per_device, :]
            qtmp_ref[d, r:r + per_device, :] = (
                x * c + pltpu.roll(x, HD // 2, 1) * (s * sign[:1])
            ) * scale
    lane_r = lax.broadcasted_iota(jnp.int32, (rp, LANES), 1)
    for d in range(n_dest):
        x = qtmp_ref[d]
        z = jnp.where(lane_r < HD // 2, 1.0, -1.0) * pltpu.roll(x, HD // 2, 1)
        hi, lo = split2(jnp.concatenate([x, z], 1))
        qs_ref[d] = jnp.concatenate([hi, lo], 0)

    for c in o_copies:
        c.wait()
    x_rows = kx_ref.shape[1]
    for g in range(KVH):
        sl = slice(g * HD, (g + 1) * HD)
        xtmp_ref[...] = jnp.zeros_like(xtmp_ref)
        for j in range(OMOST):
            wide = okeys_ref[j, :, sl].astype(F32)
            x = jnp.where(o_span[j] % 2 == 0, wide[:8], wide[8:])
            rows = pl.ds(pl.multiple_of(o_span[j] * SPAN, SPAN), SPAN)
            xtmp_ref[j * SPAN:(j + 1) * SPAN, :] = turn(x, cc_ref[rows, :], ss_ref[rows, :])
        x = fk_ref[:, sl].astype(F32)
        o = OMOST * SPAN
        xtmp_ref[o:o + steps, :] = x * cq_ref[:steps, :] + pltpu.roll(x, HD // 2, 1) * (sq_ref[:steps, :] * sign[:1])
        kx_ref[g, :, :HD] = xtmp_ref[...].astype(BF)
        kx_ref[g, :, HD:] = jnp.zeros((x_rows, HD), BF)

    for c in copies:
        c.wait()
    vtmp_ref[...] = jnp.zeros_like(vtmp_ref)
    live_ref[steps * KVH] = o_here
    live_ref[steps * KVH + 1] = me
    sel = chosen_ref.shape[1]
    part = 16 if most % 16 == 0 else 8

    def value_rows(span, lanes):
        wide = values_ref[pl.ds(pl.multiple_of(span // 2 * 16, 16), 16), lanes].astype(F32)
        return jnp.where(span % 2 == 0, wide[:8], wide[8:])

    for g in range(KVH):
        lanes = slice(g * HD, (g + 1) * HD)
        for j in range(OMOST):
            o = tok_main + j * SPAN
            vtmp_ref[o:o + SPAN, :] = value_rows(o_span[j], lanes)
        o = tok_main + OMOST * SPAN
        vtmp_ref[o:o + steps, :] = fv_ref[:, lanes].astype(F32)

        def one_list(t, _, g=g, lanes=lanes):
            i = t * KVH + g
            start = lax.fori_loop(0, me, lambda r, s: s + counts_ref[i, r], jnp.int32(0))
            count = counts_ref[i, me]
            live_ref[i] = count
            for k in range(most // part):
                @pl.when(k * part < count)
                def _():
                    for j in range(k * part, (k + 1) * part):
                        picked = chosen_ref[i, jnp.minimum(start + j, sel - 1)]
                        span = jnp.clip(picked - base, 0, spans - 1)
                        slots_ref[i, j] = span
                        o = j * SPAN if j * SPAN < tok_main else j * SPAN + LANES
                        vtmp_ref[o:o + SPAN, :] = value_rows(span, lanes)
            vg_ref[i] = vtmp_ref[...].astype(BF)
            return 0

        lax.fori_loop(0, steps, one_list, 0)


def attend_kernel(
    core_ref, slots_ref, live_ref, zmine_ref, zother_ref, kx_ref, qs_ref,
    keys_hbm, cc_hbm, ss_hbm, vg_hbm,
    kft_hbm, out_ref,
    keys_ref, cc_ref, ss_ref, vg_ref, z_ref, a_ref, qt_ref, kf_ref, kft_ref, kg_ref, cg_ref, sg_ref, sc_ref,
    sem, out_sem, *, most, per_device, steps, tok_main
):
    rank, width = z_ref.shape
    half = rank // 2
    seq_len = keys_ref.shape[0]
    loads = [
        pltpu.make_async_copy(keys_hbm, keys_ref, sem.at[0]),
        pltpu.make_async_copy(cc_hbm, cc_ref, sem.at[1]),
        pltpu.make_async_copy(ss_hbm, ss_ref, sem.at[2]),
        pltpu.make_async_copy(vg_hbm, vg_ref, sem.at[3]),
    ]
    for c in loads:
        c.start()

    core = core_ref[0] % 2
    z_ref[pl.ds(pl.multiple_of(core * half, 16), half), :] = zmine_ref[...]
    z_ref[pl.ds(pl.multiple_of((1 - core) * half, 16), half), :] = zother_ref[...]
    basis(z_ref, a_ref, qt_ref)
    qt = qt_ref[...]

    loads[0].wait()
    chunk = 512 if seq_len % 512 == 0 else seq_len
    stores = []
    for i in range(seq_len // chunk):
        rows = keys_ref[i * chunk:(i + 1) * chunk, :]
        kf_ref[i * chunk:(i + 1) * chunk, :] = lax.dot_general(rows, qt, NT, preferred_element_type=F32)
        kft_ref[:, i * chunk:(i + 1) * chunk] = lax.dot_general(qt, rows, NT, preferred_element_type=F32)
    store = pltpu.make_async_copy(kft_ref, kft_hbm, out_sem)
    store.start()

    loads[1].wait()
    loads[2].wait()
    n_lists = steps * KVH
    part = 8

    def gather_list(i, _):
        count = live_ref[i]

        def gather_part(k, _):
            for j in range(part):
                slot = k * part + j
                src = pl.ds(pl.multiple_of(slots_ref[i, slot] * SPAN, SPAN), SPAN)
                dst = pl.ds(pl.multiple_of(slot * SPAN, SPAN), SPAN)
                kg_ref[i, dst, :] = kf_ref[src, :]
                cg_ref[i, dst, :] = cc_ref[src, :]
                sg_ref[i, dst, :] = ss_ref[src, :]
            return 0

        lax.fori_loop(0, (count + part - 1) // part, gather_part, 0)
        return 0

    lax.fori_loop(0, n_lists, gather_list, 0)

    group = QH // KVH
    dests = group // per_device
    rp = sc_ref.shape[1]
    toks = sc_ref.shape[2]
    main = min(tok_main, most * SPAN)
    sc_ref[...] = jnp.full(sc_ref.shape, DEAD, F32)
    o_live = live_ref[n_lists] * SPAN
    first_shard = live_ref[n_lists + 1] == 0

    def q_rows(g):
        hi = jnp.concatenate([qs_ref[g * dests + a, :rp] for a in range(dests)], 0)
        lo = jnp.concatenate([qs_ref[g * dests + a, rp:] for a in range(dests)], 0)
        return jnp.concatenate([hi, lo], 0)

    def slot_scores(g, t, q, lo_row, n_rows):
        i = t * KVH + g
        x = jnp.dot(
            kg_ref[i, lo_row:lo_row + n_rows, :].astype(BF), qt[:, g * HD:(g + 1) * HD], preferred_element_type=F32
        )
        y = jnp.concatenate(
            [x * cg_ref[i, lo_row:lo_row + n_rows, :], x * sg_ref[i, lo_row:lo_row + n_rows, :]], 1
        ).astype(BF)
        s = lax.dot_general(q, y, NT, preferred_element_type=F32)
        s = s[:dests * rp] + s[dests * rp:]
        lane = lax.broadcasted_iota(jnp.int32, (dests * rp, n_rows), 1) + lo_row
        return jnp.where(lane < live_ref[i] * SPAN, s, DEAD)

    def put(g, t, s, at):
        for a in range(dests):
            r = t * per_device
            sc_ref[g * dests + a, r:r + per_device, at:at + s.shape[1]] = s[a * rp + r:a * rp + r + per_device]

    for g in range(KVH):
        q = q_rows(g)
        for t in range(steps):
            put(g, t, slot_scores(g, t, q, 0, main), 0)
        s = lax.dot_general(q, kx_ref[g], NT, preferred_element_type=F32)
        s = s[:dests * rp] + s[dests * rp:]
        lane = lax.broadcasted_iota(jnp.int32, s.shape, 1)
        row = lax.broadcasted_iota(jnp.int32, s.shape, 0) % rp
        new = lane - OMOST * SPAN
        is_live = (lane < o_live) | (first_shard & (new >= 0) & (new * per_device <= row))
        is_live = is_live & (new < steps) & (row < steps * per_device)
        s = jnp.where(is_live, s, DEAD)
        for a in range(dests):
            sc_ref[g * dests + a, :, tok_main:tok_main + LANES] = s[a * rp:(a + 1) * rp]
        if most * SPAN > main:
            for t in range(steps):
                @pl.when(live_ref[t * KVH + g] * SPAN > main)
                def _():
                    put(g, t, slot_scores(g, t, q, main, most * SPAN - main), tok_main + LANES)

    loads[3].wait()
    base_toks = tok_main + LANES
    rowi = lax.broadcasted_iota(jnp.int32, (rp, LANES), 0)
    eye = rowi == lax.broadcasted_iota(jnp.int32, (rp, LANES), 1)
    used = steps * per_device
    for g in range(KVH):
        ps = []
        ms = []
        ls = []
        for a in range(dests):
            s = sc_ref[g * dests + a]
            m = jnp.max(s, axis=1, keepdims=True)
            p = jnp.where(s > 0.5 * DEAD, jnp.exp(s - m), 0.0)
            l = jnp.sum(p, axis=1, keepdims=True)
            sc_ref[g * dests + a] = p
            ps.append(p)
            ms.append(m)
            ls.append(l)
        p = jnp.concatenate(ps, 0)
        hi, lo = split2(p)
        pp = jnp.concatenate([hi, lo], 0)
        acc = jnp.zeros((dests * rp, HD), F32)
        row = lax.broadcasted_iota(jnp.int32, (dests * rp, HD), 0) % rp // per_device
        for t in range(steps):
            i = t * KVH + g
            r = jnp.dot(pp[:, :base_toks], vg_ref[i, :base_toks, :], preferred_element_type=F32)
            r = r[:dests * rp] + r[dests * rp:]
            acc = jnp.where(row == t, r, acc)
        for a in range(dests):
            d = g * dests + a
            m_row = jnp.sum(jnp.where(eye, ms[a], 0.0), axis=0, keepdims=True)
            l_row = jnp.sum(jnp.where(eye, ls[a], 0.0), axis=0, keepdims=True)
            r = acc[a * rp:(a + 1) * rp]
            out_ref[d] = jnp.where(rowi == used, m_row, jnp.where(rowi == used + 1, l_row, r))
        if toks > base_toks:
            for t in range(steps):
                @pl.when(live_ref[t * KVH + g] * SPAN > main)
                def _():
                    i = t * KVH + g
                    rs = slice(t * per_device, (t + 1) * per_device)
                    p = jnp.concatenate([sc_ref[g * dests + a, :, base_toks:] for a in range(dests)], 0)
                    hi, lo = split2(p)
                    pp = jnp.concatenate([hi, lo], 0)
                    r = jnp.dot(pp, vg_ref[i, base_toks:, :], preferred_element_type=F32)
                    r = r[:dests * rp] + r[dests * rp:]
                    for a in range(dests):
                        out_ref[g * dests + a, rs, :] += r[a * rp + rs.start:a * rp + rs.stop]
    store.wait()


def basis(z_ref, a_ref, qt_ref):
    rank = z_ref.shape[0]
    wide = round_up(rank, LANES)
    z = z_ref[...]
    c = lax.dot_general(z, z, NT, preferred_element_type=F32)
    rows = lax.broadcasted_iota(jnp.int32, (rank, wide), 0)
    cols = lax.broadcasted_iota(jnp.int32, (rank, wide), 1)
    a_ref[:, :wide] = jnp.where(rows == cols, 1.0, 0.0)
    a_ref[:, wide:wide + rank] = c
    a_ref[:, wide + rank:] = jnp.zeros((rank, wide - rank), F32)
    nb = 32
    half_tiles = wide // LANES
    for j0 in range(0, rank, nb):
        tiles = [t for t in range(half_tiles) if t * LANES < j0 + nb]
        tiles += [half_tiles + t for t in range(half_tiles) if (t + 1) * LANES > j0]
        part = {t: a_ref[j0:j0 + nb, t * LANES:(t + 1) * LANES] for t in tiles}
        row = lax.broadcasted_iota(jnp.int32, (nb, LANES), 0)
        column = []
        for j in range(nb):
            t, o = divmod(j0 + j, LANES)
            column.append(jnp.broadcast_to(part[half_tiles + t][:, o:o + 1], (nb, LANES)))
        for j in range(nb):
            inverse = lax.rsqrt(jnp.broadcast_to(column[j][j:j + 1, :], (nb, LANES)))
            low = jnp.where(row > j, column[j] * inverse, 0.0)
            for k in range(j + 1, nb):
                column[k] = column[k] - low * jnp.broadcast_to(low[k:k + 1, :], (nb, LANES))
            for t in tiles:
                upper = jnp.broadcast_to(part[t][j:j + 1, :], (nb, LANES)) * inverse
                part[t] = jnp.where(row == j, upper, part[t] - low * upper)
        for t in tiles:
            a_ref[j0:j0 + nb, t * LANES:(t + 1) * LANES] = part[t]
        if j0 + nb < rank:
            upper = jnp.concatenate(
                [part[t] if t in part else jnp.zeros((nb, LANES), F32) for t in range(2 * half_tiles)], 1
            )
            h, m, l = split3(upper)
            left = jnp.concatenate([h, h, m, m, h, l], 0)[:, wide:].astype(BF)
            right = jnp.concatenate([h, m, h, m, l, h], 0).astype(BF)
            for s in range(2):
                d = lax.dot_general(left, right[:, s * wide:(s + 1) * wide], TN, preferred_element_type=F32)
                a_ref[j0 + nb:, s * wide:(s + 1) * wide] -= d[j0 + nb:rank]
    h, m, _ = split3(a_ref[:, :rank])
    q = jnp.dot(jnp.concatenate([h, m], 0).astype(BF), z, preferred_element_type=F32)
    qt_ref[...] = (q[:rank] + q[rank:]).astype(BF)


def merge_kernel(parts_ref, out_ref, *, steps, per_device):
    n, rp, _ = parts_ref.shape
    used = steps * per_device
    eye = lax.broadcasted_iota(jnp.int32, (rp, LANES), 0) == lax.broadcasted_iota(jnp.int32, (rp, LANES), 1)

    def column(s, r):
        return jnp.sum(jnp.where(eye, parts_ref[s, r:r + 1, :], 0.0), axis=1, keepdims=True)

    ms = [column(s, used) for s in range(n)]
    top = functools.reduce(jnp.maximum, ms)
    total = jnp.zeros((rp, 1), F32)
    acc = jnp.zeros((rp, HD), F32)
    for s in range(n):
        w = jnp.exp(ms[s] - top)
        total = total + w * column(s, used + 1)
        acc = acc + w * parts_ref[s]
    o = acc / total
    for t in range(steps):
        for i in range(per_device):
            r = t * per_device + i
            out_ref[t:t + 1, i * HD:(i + 1) * HD] = o[r:r + 1, :].astype(BF)


def swap(x, moves):
    return lax.ppermute(x, "seq", moves)


def on_device(
    cache_keys,
    cache_values,
    sketch_matrix,
    queries,
    fresh_keys,
    fresh_values,
    chosen,
    shard_counts,
    outliers,
):
    seq_len, width = cache_keys.shape
    devices = lax.axis_size("seq")
    myself = lax.axis_index("seq")
    length = seq_len * devices
    steps = queries.shape[0]
    rank = sketch_matrix.shape[1]
    per_device = QH // devices
    n_lists = steps * KVH
    most = 3 * chosen.shape[2] // devices
    tok_sel = most * SPAN
    tok_main = min(256, round_up(tok_sel, LANES))
    toks = tok_main + LANES + max(0, round_up(tok_sel - tok_main, LANES))
    used = steps * per_device
    rp = round_up(used + 2, 8)
    me = jnp.full((1,), myself, jnp.int32)

    keep, send = sketch_share(me, sketch_matrix.T, cache_keys, length)

    half_width = HD // 2
    exponents = jnp.arange(half_width, dtype=F32) * (2.0 / HD)
    inverse_freq = jnp.exp(-jnp.log(F32(500000.0)) * exponents)
    inverse_freq = jnp.concatenate([inverse_freq, inverse_freq])
    blk = 64
    coarse = (myself * seq_len + blk * jnp.arange(seq_len // blk, dtype=jnp.int32)).astype(F32)[:, None] * inverse_freq
    fine = jnp.arange(blk, dtype=jnp.int32).astype(F32)[:, None] * inverse_freq
    late = (length + jnp.arange(steps, dtype=jnp.int32)).astype(F32)[:, None] * inverse_freq

    x_rows = LANES
    table = jax.ShapeDtypeStruct((seq_len, HD), F32)
    n_chunks = 8 if seq_len % 128 == 0 else 1
    n_dest = devices
    slots, live, cc, ss, vg, kx, qs = pl.pallas_call(
        functools.partial(
            prepare_kernel, most=most, per_device=per_device, tok_sel=tok_sel, tok_main=tok_main
        ),
        in_specs=[smem()] * 4 + [vmem()] * 9 + [hbm()] * 2,
        out_specs=[smem()] * 2 + [vmem()] * 5,
        out_shape=[
            jax.ShapeDtypeStruct((n_lists, most), jnp.int32),
            jax.ShapeDtypeStruct((n_lists + 2,), jnp.int32),
            table,
            table,
            jax.ShapeDtypeStruct((n_lists, toks, HD), BF),
            jax.ShapeDtypeStruct((KVH, x_rows, 2 * HD), BF),
            jax.ShapeDtypeStruct((n_dest, 2 * rp, 2 * HD), BF),
        ],
        scratch_shapes=[
            pltpu.VMEM((seq_len, width), BF),
            pltpu.VMEM((OMOST, 16, width), BF),
            pltpu.VMEM((toks, HD), F32),
            pltpu.VMEM((x_rows, HD), F32),
            pltpu.VMEM((n_dest, rp, HD), F32),
            pltpu.SemaphoreType.DMA((n_chunks,)),
            pltpu.SemaphoreType.DMA((OMOST,)),
        ],
        compiler_params=pltpu.CompilerParams(vmem_limit_bytes=48 << 20),
        name="prepare",
    )(
        me, chosen.reshape(n_lists, -1), shard_counts.reshape(n_lists, -1), outliers,
        queries, fresh_keys, fresh_values,
        jnp.cos(coarse), jnp.sin(coarse), jnp.cos(fine), jnp.sin(fine), jnp.cos(late), jnp.sin(late),
        cache_keys, cache_values,
    )

    z = keep + swap(send, [(i, i ^ 1) for i in range(devices)])
    hops = [1 << k for k in range(1, devices.bit_length() - 1)]
    for k in range(len(hops)):
        other = k ^ 1 if k < 2 and len(hops) >= 2 else k
        moves = [(i, i ^ hops[k if i % 2 == 0 else other]) for i in range(devices)]
        z = z + swap(z.astype(BF), moves).astype(F32)
    z = z.astype(BF)
    z_other = swap(z, [(i, i ^ 1) for i in range(devices)])

    kft, parts = pl.pallas_call(
        functools.partial(
            attend_kernel, most=most, per_device=per_device, steps=steps, tok_main=tok_main
        ),
        in_specs=[smem()] * 3 + [vmem()] * 4 + [hbm()] * 4,
        out_specs=[hbm(), vmem()],
        out_shape=[
            jax.ShapeDtypeStruct((rank, seq_len), F32),
            jax.ShapeDtypeStruct((n_dest, rp, HD), F32),
        ],
        scratch_shapes=[
            pltpu.VMEM((seq_len, width), BF),
            pltpu.VMEM((seq_len, HD), F32),
            pltpu.VMEM((seq_len, HD), F32),
            pltpu.VMEM((n_lists, toks, HD), BF),
            pltpu.VMEM((rank, width), BF),
            pltpu.VMEM((rank, 2 * round_up(rank, LANES)), F32),
            pltpu.VMEM((rank, width), BF),
            pltpu.VMEM((seq_len, rank), F32),
            pltpu.VMEM((rank, seq_len), F32),
            pltpu.VMEM((n_lists, tok_sel, rank), F32),
            pltpu.VMEM((n_lists, tok_sel, HD), F32),
            pltpu.VMEM((n_lists, tok_sel, HD), F32),
            pltpu.VMEM((n_dest, rp, toks), F32),
            pltpu.SemaphoreType.DMA((4,)),
            pltpu.SemaphoreType.DMA,
        ],
        compiler_params=pltpu.CompilerParams(vmem_limit_bytes=60 << 20),
        name="attend",
    )(me, slots, live, z, z_other, kx, qs, cache_keys, cc, ss, vg)

    parts = lax.all_to_all(parts, "seq", 0, 0, tiled=True)
    attended = pl.pallas_call(
        functools.partial(merge_kernel, steps=steps, per_device=per_device),
        in_specs=[vmem()],
        out_specs=vmem(),
        out_shape=jax.ShapeDtypeStruct((steps, per_device * HD), BF),
        name="merge",
    )(parts)
    return (attended, kft.T)


def solution(mesh):
    in_specs = (
        P(("groups", "seq"), None),
        P(("groups", "seq"), None),
        P(),
        P("groups", None),
        P("groups", None),
        P("groups", None),
        P("groups", None, None),
        P("groups", None, None),
        P("groups"),
    )
    out_specs = (P("groups", "seq"), P(("groups", "seq"), None))
    return jax.shard_map(
        on_device, mesh=mesh, in_specs=in_specs, out_specs=out_specs, check_vma=False
    )
```

time: 304 us -> 95.9 us (0.32); the launches traced: 299 us -> 96.1 us
  other arithmetic: 89.4 us -> 0.74 us
  matrix products: 45.9 us -> 0 us
  local copies, waits for them, and re-layouts: 51.8 us -> 10.6 us
  Pallas kernels: 0 us -> 40.3 us
  blocking collectives: 60.2 us -> 21 us
  waiting for transfers between devices: 35.1 us -> 13.7 us
  between operations: 16 us -> 0.84 us
  starting transfers between devices: 0.08 us -> 8.78 us
    another operation x19 -> x0, other arithmetic: 66.9 us -> none  [the longest x7 25.8 us: make_basis(): lower = jnp.linalg.cholesky(small_gram)]
    all_gather x3 -> x0, blocking collectives: 60.2 us -> none  [the longest x2 37.6 us: merged_2(): everything = jax.tree.map(lambda part: lax.all_gather(part, axis), x)]
    gather x8 -> x0, local copies, waits for them, and re-layouts: 43.8 us -> none  [the longest x1 15 us: on_device(): sel_values = value_blocks[local_span, :, head_ids[None, :, None], :]]
    dot_general x9 -> x0, matrix products: 43.3 us -> none  [the longest x1 15.1 us: on_device(): lax.dot_general(cache_keys, cache_keys, contract, preferred_element_type=...]
    pallas_call x0 -> x4, Pallas kernels: none -> 40.3 us  [the longest x1 21 us: on_device(): pl.pallas_call(functools.partial(attend_kernel, most=most, per_device=per...]
    reduce_scatter x1 -> x0, waiting for transfers between devices: 35 us -> none  [on_device(): lax.psum_scatter(lax.dot_general(cache_keys, cache_keys, contract, prefer...]
    all_to_all x0 -> x1, blocking collectives: none -> 21 us  [on_device(): parts = lax.all_to_all(parts, 'seq', 0, 0, tiled=True)]
    add x31 -> x0, other arithmetic: 16 us -> none  [the longest x15 15.6 us: combine(): earlier[2] * scale_early[..., None] + later[2] * scale_late[..., None]]
  transfers between devices with their start and end apart: 2 -> 5, of which waited for: 1 -> 4; matrix products, arithmetic and copies ran while one was open for 14% -> 1% of each run, Pallas kernels for 0% -> 13%
where the time goes in v1:
time: 95.9 us; the launch traced here: 96.1 us
  Pallas kernels  40.3 us (42%)
  blocking collectives  21 us (22%)
  waiting for transfers between devices  13.7 us (14%)
  local copies, waits for them, and re-layouts  10.6 us (11%)
  starting transfers between devices  8.78 us (9%)
    all_to_all x1, blocking collectives, on_device(): parts = lax.all_to_all(parts, 'seq', 0, 0, tiled=True)  21 us
    pallas_call x1, Pallas kernels, on_device(): pl.pallas_call(functools.partial(attend_kernel, most=most, per_device=per...  21 us
    ppermute x5, waiting for transfers between devices, swap(): return lax.ppermute(x, 'seq', moves)  13.7 us
    pallas_call x1, Pallas kernels, on_device(): pl.pallas_call(functools.partial(prepare_kernel, most=most, per_device=pe...  12.3 us
    unnamed x32, local copies, waits for them, and re-layouts  10.6 us
    ppermute x5, starting transfers between devices, swap(): return lax.ppermute(x, 'seq', moves)  8.78 us
    pallas_call x1, Pallas kernels, sketch_share(): pl.pallas_call(functools.partial(sketch_kernel, scale=1.0 / length, chunk...  5.4 us
  transfers between devices with their start and end apart: 5, of which 4 were waited for; matrix products, arithmetic and copies ran while one was open for 1% of the time, Pallas kernels for 13%

profile of v1, /device:TPU:0, one launch (start us, length us, event | category | flops | bytes accessed | tf_op | source)
XLA Modules:
  0.0 96.1 jit_solution(12013735417501501884)
XLA Ops:
  0.6 0.0 copy-start
  0.6 3.4 %copy-done = bf16[4096,1024]{1,0:T(8,128)(2,1)S(1)} copy-done((bf16[4096,1024]{1,0:T(8,128)(2,1)S(1)}, bf16[4096,1024]{1,0:T(8,128)(2,1)}, u32[]{:S(2)}) %copy-start) | copy-done | bytes 8388632
  4.0 0.0 copy-start.3
  4.0 1.1 %copy-done.3 = f32[1024,160]{0,1:T(8,128)S(1)} copy-done((f32[1024,160]{0,1:T(8,128)S(1)}, f32[1024,160]{0,1:T(8,128)}, u32[]{:S(2)}) %copy-start.3) | copy-done | bytes 655384
  5.1 5.4 %sketch_share.1 = (f32[80,1024]{1,0:T(8,128)S(1)}, f32[80,1024]{1,0:T(8,128)S(1)}) custom-call(s32[1]{0:T(128)} %bitcast.me_ref.core_ref, f32[160,1024]{1,0:T(8,128)S(1)} %bitcast.5, bf16[4096,1024]{1,0:T(8,128)(2,1)S(1)} %copy-done), custom_call_target="tpu_custom_call" | custom-call | tf_op jit(solution)/shard_map/sketch_share/pallas_call | solution.py:97
  10.5 0.0 copy-start.6
  10.5 0.0 copy-start.7
  10.5 0.0 copy-start.8
  10.5 0.0 copy-start.10
  10.6 0.0 copy-start.11
  10.6 0.0 copy-start.12
  10.6 0.5 collective-permute-start
  11.1 1.3 %collective-permute-done = f32[80,1024]{1,0:T(8,128)S(1)} collective-permute-done((f32[80,1024]{1,0:T(8,128)S(1)}, f32[80,1024]{1,0:T(8,128)S(1)}, u32[]{:S(2)}, u32[]{:S(2)}) %collective-permute-start) | collective-permute-done | bytes 327712 | tf_op jit(solution)/shard_map/ppermute | solution.py:482
  12.4 3.0 %collective-permute-start.1 = (bf16[80,1024]{1,0:T(8,128)(2,1)S(1)}, bf16[80,1024]{1,0:T(8,128)(2,1)S(1)}, u32[]{:S(2)}, u32[]{:S(2)}) collective-permute-start(bf16[80,1024]{1,0:T(8,128)(2,1)S(1)} %get-tuple-element.24), channel_id=1, source_target_pairs={{0,2},{1,5},{2,0},{3,7},{4,6},{5,1},{6,4},{7,3},{8,10},{9,13},{10,... | collective-permute-start | bytes 491528 | tf_op jit(solution)/shard_map/ppermute | solution.py:482
  15.4 3.3 %collective-permute-done.1 = bf16[80,1024]{1,0:T(8,128)(2,1)S(1)} collective-permute-done((bf16[80,1024]{1,0:T(8,128)(2,1)S(1)}, bf16[80,1024]{1,0:T(8,128)(2,1)S(1)}, u32[]{:S(2)}, u32[]{:S(2)}) %collective-permute-start.1) | collective-permute-done | bytes 163872 | tf_op jit(solution)/shard_map/ppermute | solution.py:482
  18.7 2.1 %collective-permute-start.2 = (bf16[80,1024]{1,0:T(8,128)(2,1)S(1)}, bf16[80,1024]{1,0:T(8,128)(2,1)S(1)}, u32[]{:S(2)}, u32[]{:S(2)}) collective-permute-start(bf16[80,1024]{1,0:T(8,128)(2,1)S(1)} %fusion), channel_id=1, source_target_pairs={{0,4},{1,3},{2,6},{3,1},{4,0},{5,7},{6,2},{7,5},{8,12},{9,11},{10,... | collective-permute-start | bytes 491528 | tf_op jit(solution)/shard_map/ppermute | solution.py:482
  20.8 0.1 pad_maximum_fusion
  20.9 3.2 %collective-permute-done.2 = bf16[80,1024]{1,0:T(8,128)(2,1)S(1)} collective-permute-done((bf16[80,1024]{1,0:T(8,128)(2,1)S(1)}, bf16[80,1024]{1,0:T(8,128)(2,1)S(1)}, u32[]{:S(2)}, u32[]{:S(2)}) %collective-permute-start.2) | collective-permute-done | bytes 163872 | tf_op jit(solution)/shard_map/ppermute | solution.py:482
  24.1 0.1 fusion.1
  24.2 3.1 %collective-permute-start.3 = (bf16[80,1024]{1,0:T(8,128)(2,1)S(1)}, bf16[80,1024]{1,0:T(8,128)(2,1)S(1)}, u32[]{:S(2)}, u32[]{:S(2)}) collective-permute-start(bf16[80,1024]{1,0:T(8,128)(2,1)S(1)} %fusion.1), channel_id=1, source_target_pairs={{0,8},{1,9},{2,10},{3,11},{4,12},{5,13},{6,14},{7,15},{8,0},{9,1},... | collective-permute-start | bytes 491528 | tf_op jit(solution)/shard_map/ppermute | solution.py:482
  27.3 0.3 multiply_sine_fusion
  27.6 6.0 %collective-permute-done.3 = bf16[80,1024]{1,0:T(8,128)(2,1)S(1)} collective-permute-done((bf16[80,1024]{1,0:T(8,128)(2,1)S(1)}, bf16[80,1024]{1,0:T(8,128)(2,1)S(1)}, u32[]{:S(2)}, u32[]{:S(2)}) %collective-permute-start.3) | collective-permute-done | bytes 163872 | tf_op jit(solution)/shard_map/ppermute | solution.py:482
  33.6 0.1 add_convert_fusion.zmine_ref
  33.7 0.0 copy-start.14
  33.7 0.1 collective-permute-start.4
  33.8 0.1 multiply_sine_fusion.2
  33.9 0.0 copy-done.6
  33.9 0.0 copy-done.7
  33.9 0.0 copy-done.8
  33.9 0.0 copy-done.10
  33.9 0.0 copy-done.11
  33.9 0.0 copy-done.12
  33.9 12.3 %prepare.1 = (s32[24,48]{1,0:T(8,128)S(1)}, s32[26]{0:T(128)S(1)}, f32[4096,128]{1,0:T(8,128)S(1)}, f32[4096,128]{1,0:T(8,128)S(1)}, bf16[24,512,128]{2,1,0:T(8,...) custom-call(s32[1]{0:T(128)} %bitcast.me_ref.core_ref, s32[24,256]{1,0:T(8,128)S(1)} %bitcast.6, ...), custom_call_target="tpu_custom_call" | custom-call | tf_op jit(solution)/shard_map/prepare/pallas_call | solution.py:527
  46.2 0.0 copy-done.14
  46.2 0.0 copy-start.1
  46.3 1.4 %copy-done.1 = f32[4096,128]{1,0:T(8,128)} copy-done((f32[4096,128]{1,0:T(8,128)}, f32[4096,128]{1,0:T(8,128)S(1)}, u32[]{:S(2)}) %copy-start.1) | copy-done | bytes 2097176
  47.6 0.0 copy-start.2
  47.6 1.3 %copy-done.2 = f32[4096,128]{1,0:T(8,128)} copy-done((f32[4096,128]{1,0:T(8,128)}, f32[4096,128]{1,0:T(8,128)S(1)}, u32[]{:S(2)}) %copy-start.2) | copy-done | bytes 2097176
  49.0 0.0 copy-start.4
  49.0 0.8 copy-done.4
  49.8 0.7 copy-done.5
  50.5 0.6 copy-done.9
  51.1 0.6 copy-done.13
  51.7 0.0 collective-permute-done.4.zother_ref
  51.7 0.7 copy-done.15
  52.3 21.0 %attend.1 = (f32[160,4096]{1,0:T(8,128)}, f32[16,16,128]{2,1,0:T(8,128)}) custom-call(s32[1]{0:T(128)} %bitcast.me_ref.core_ref, s32[24,48]{1,0:T(8,128)} %copy-done.9, s32[26]{0:T(128)} %copy-done.13, bf16[80,1024]{1,0:T(8,128)(2,1)} %copy-done.14, bf16[80,1024]{1,0:T(8,128)(2,1)} %copy-done.15, bf16[8,128,256]{2,1,0:T(8,128)(2,1)} %copy-done.4, ...), custom_call_target="tpu_custom_call" | custom-call | tf_op jit(solution)/shard_map/attend/pallas_call | solution.py:569
  73.4 21.0 %all_to_all.5.parts_ref = f32[16,16,128]{2,1,0:T(8,128)} all-to-all(f32[16,16,128]{2,1,0:T(8,128)} %get-tuple-element.22), channel_id=1, replica_groups=mesh['groups'=2,'seq'=16] {'seq'}, dimensions={0} | all-to-all | bytes 262144 | tf_op jit(solution)/shard_map/all_to_all | solution.py:600
  94.4 1.7 %merge.1 = bf16[3,512]{1,0:T(4,128)(2,1)} custom-call(f32[16,16,128]{2,1,0:T(8,128)} %all_to_all.5.parts_ref), custom_call_target="tpu_custom_call" | custom-call | tf_op jit(solution)/shard_map/merge/pallas_call | solution.py:601
  (10 shorter events, 0.1 us)
Async XLA Ops:
  0.6 3.4 %copy-start = (bf16[4096,1024]{1,0:T(8,128)(2,1)S(1)}, bf16[4096,1024]{1,0:T(8,128)(2,1)}, u32[]{:S(2)}) copy-start(bf16[4096,1024]{1,0:T(8,128)(2,1)} %keys_hbm.5) | copy-start | bytes 25165828
  4.0 1.1 %copy-start.3 = (f32[1024,160]{0,1:T(8,128)S(1)}, f32[1024,160]{0,1:T(8,128)}, u32[]{:S(2)}) copy-start(f32[1024,160]{0,1:T(8,128)} %param.11) | copy-start | bytes 1966084
  10.5 23.4 %copy-start.6 = (bf16[3,8192]{1,0:T(4,128)(2,1)S(1)}, bf16[3,8192]{1,0:T(4,128)(2,1)}, u32[]{:S(2)}) copy-start(bf16[3,8192]{1,0:T(4,128)(2,1)} %q_ref.1) | copy-start | bytes 147460
  10.5 23.4 %copy-start.7 = (s32[3,8,256]{2,1,0:T(8,128)S(1)}, s32[3,8,256]{2,1,0:T(8,128)}, u32[]{:S(2)}) copy-start(s32[3,8,256]{2,1,0:T(8,128)} %param.15) | copy-start | bytes 73732
  10.5 23.4 %copy-start.8 = (s32[3,8,16]{2,1,0:T(8,128)S(1)}, s32[3,8,16]{2,1,0:T(8,128)}, u32[]{:S(2)}) copy-start(s32[3,8,16]{2,1,0:T(8,128)} %param.16) | copy-start | bytes 4612
  10.5 23.4 %copy-start.10 = (bf16[3,1024]{1,0:T(4,128)(2,1)S(1)}, bf16[3,1024]{1,0:T(4,128)(2,1)}, u32[]{:S(2)}) copy-start(bf16[3,1024]{1,0:T(4,128)(2,1)} %fk_ref.1) | copy-start | bytes 18436
  10.6 23.4 %copy-start.11 = (bf16[3,1024]{1,0:T(4,128)(2,1)S(1)}, bf16[3,1024]{1,0:T(4,128)(2,1)}, u32[]{:S(2)}) copy-start(bf16[3,1024]{1,0:T(4,128)(2,1)} %fv_ref.1) | copy-start | bytes 18436
  10.6 23.4 %copy-start.12 = (s32[32]{0:T(128)S(1)}, s32[32]{0:T(128)}, u32[]{:S(2)}) copy-start(s32[32]{0:T(128)} %outl_ref.1) | copy-start | bytes 388
  10.6 1.8 %collective-permute-start = (f32[80,1024]{1,0:T(8,128)S(1)}, f32[80,1024]{1,0:T(8,128)S(1)}, u32[]{:S(2)}, u32[]{:S(2)}) collective-permute-start(f32[80,1024]{1,0:T(8,128)S(1)} %get-tuple-element.16), channel_id=1, source_target_pairs={{0,1},{1,0},{2,3},{3,2},{4,5},{5,4},{6,7},{7,6},{8,9},{9,8},{10,11... | collective-permute-start | bytes 983048 | tf_op jit(solution)/shard_map/ppermute | solution.py:482
  12.4 6.3 %collective-permute-start.1 = (bf16[80,1024]{1,0:T(8,128)(2,1)S(1)}, bf16[80,1024]{1,0:T(8,128)(2,1)S(1)}, u32[]{:S(2)}, u32[]{:S(2)}) collective-permute-start(bf16[80,1024]{1,0:T(8,128)(2,1)S(1)} %get-tuple-element.24), channel_id=1, source_target_pairs={{0,2},{1,5},{2,0},{3,7},{4,6},{5,1},{6,4},{7,3},{8,10},{9,13},{10,... | collective-permute-start | bytes 491528 | tf_op jit(solution)/shard_map/ppermute | solution.py:482
  18.7 5.4 %collective-permute-start.2 = (bf16[80,1024]{1,0:T(8,128)(2,1)S(1)}, bf16[80,1024]{1,0:T(8,128)(2,1)S(1)}, u32[]{:S(2)}, u32[]{:S(2)}) collective-permute-start(bf16[80,1024]{1,0:T(8,128)(2,1)S(1)} %fusion), channel_id=1, source_target_pairs={{0,4},{1,3},{2,6},{3,1},{4,0},{5,7},{6,2},{7,5},{8,12},{9,11},{10,... | collective-permute-start | bytes 491528 | tf_op jit(solution)/shard_map/ppermute | solution.py:482
  24.2 9.4 %collective-permute-start.3 = (bf16[80,1024]{1,0:T(8,128)(2,1)S(1)}, bf16[80,1024]{1,0:T(8,128)(2,1)S(1)}, u32[]{:S(2)}, u32[]{:S(2)}) collective-permute-start(bf16[80,1024]{1,0:T(8,128)(2,1)S(1)} %fusion.1), channel_id=1, source_target_pairs={{0,8},{1,9},{2,10},{3,11},{4,12},{5,13},{6,14},{7,15},{8,0},{9,1},... | collective-permute-start | bytes 491528 | tf_op jit(solution)/shard_map/ppermute | solution.py:482
  33.7 12.5 %copy-start.14 = (bf16[80,1024]{1,0:T(8,128)(2,1)}, bf16[80,1024]{1,0:T(8,128)(2,1)S(1)}, u32[]{:S(2)}) copy-start(bf16[80,1024]{1,0:T(8,128)(2,1)S(1)} %add_convert_fusion.zmine_ref) | copy-start | bytes 491524
  33.7 18.0 %collective-permute-start.4 = (bf16[80,1024]{1,0:T(8,128)(2,1)S(1)}, bf16[80,1024]{1,0:T(8,128)(2,1)S(1)}, u32[]{:S(2)}, u32[]{:S(2)}) collective-permute-start(bf16[80,1024]{1,0:T(8,128)(2,1)S(1)} %add_convert_fusion.zmine_ref), channel_id=1, source_target_pairs={{0,1},{1,0},{2,3},{3,2},{4,5},{5,4},{6,7},{7,6},{8,9},{9,8},{10,11... | collective-permute-start | bytes 491528 | tf_op jit(solution)/shard_map/ppermute | solution.py:482
  46.2 1.4 %copy-start.1 = (f32[4096,128]{1,0:T(8,128)}, f32[4096,128]{1,0:T(8,128)S(1)}, u32[]{:S(2)}) copy-start(f32[4096,128]{1,0:T(8,128)S(1)} %get-tuple-element.19.cc_hbm) | copy-start | bytes 6291460
  47.6 1.3 %copy-start.2 = (f32[4096,128]{1,0:T(8,128)}, f32[4096,128]{1,0:T(8,128)S(1)}, u32[]{:S(2)}) copy-start(f32[4096,128]{1,0:T(8,128)S(1)} %get-tuple-element.20.ss_hbm) | copy-start | bytes 6291460
  49.0 0.8 copy-start.4
  49.7 0.7 copy-start.5
  50.5 0.6 copy-start.9
  51.1 0.6 copy-start.13
  51.7 0.7 copy-start.15
